TPU v7x, 32 devices: a whole 2x2x4 slice. The times are simulated.
32 devices in a mesh: row: 4 (over y, x), col: 8 (over z, core).
Axes of the slice: x: 2, y: 2, z: 4, core: 2. Of those that a mesh axis runs over, the one named last changes fastest.
Arguments:
- pair_map: bfloat16 [640, 640, 128], P('row', 'col'), may hold values from -9 to 9
- input_gain: float32 [128], replicated, may hold values from 0.25 to 1.75
- input_bias: float32 [128], replicated, may hold values from -2.5 to 2.5
- left_weight: bfloat16 [128, 256], replicated, may hold values from -0.5 to 0.5
- left_bias: float32 [256], replicated, may hold values from -2.5 to 2.5
- right_weight: bfloat16 [128, 256], replicated, may hold values from -0.5 to 0.5
- right_bias: float32 [256], replicated, may hold values from -2.5 to 2.5
- gate_weight: bfloat16 [128, 128], replicated, may hold values from -0.5 to 0.5
- gate_bias: float32 [128], replicated, may hold values from -2.5 to 2.5
- output_gain: float32 [128], replicated, may hold values from 0.25 to 1.75
- output_bias: float32 [128], replicated, may hold values from -2.5 to 2.5
- final_weight: bfloat16 [128, 128], replicated, may hold values from -0.5 to 0.5
- final_bias: float32 [128], replicated, may hold values from -2.5 to 2.5
Outputs:
- slab_update: bfloat16 [8, 640, 128], P('row', 'col')
All inputs are finite; a program needn't handle non-finite values.
Results may differ from a plain program's by a relative error of at most 0.014.
Values may be sent and summed in bfloat16 or wider, within the bound.
A program may use at most 128 MiB of HBM per device.

v0:
```python
import jax
import jax.numpy as jnp
from jax import lax
from jax.sharding import PartitionSpec as P

SLAB_PER = 1


epsilon = 1e-05


def layer_norm(values, factor, offset):
    values = values.astype(jnp.float32)
    center = jnp.mean(values, axis=-1, keepdims=True)
    spread = jnp.mean(jnp.square(values - center), axis=-1, keepdims=True)
    return (values - center) * lax.rsqrt(spread + epsilon) * factor + offset


def linear(normed, weight, offset):
    flattened = normed.reshape(-1, normed.shape[-1])
    result = jnp.dot(flattened, weight, preferred_element_type=jnp.float32) + offset
    return result.reshape(normed.shape[:-1] + (weight.shape[1],))


def gated_linear(normed, weight, offset):
    joined = linear(normed, weight, offset)
    middle = weight.shape[1] // 2
    return (jax.nn.sigmoid(joined[..., middle:]) * joined[..., :middle]).astype(jnp.bfloat16)


def body(
    pair_map,
    input_gain,
    input_bias,
    left_weight,
    left_bias,
    right_weight,
    right_bias,
    gate_weight,
    gate_bias,
    output_gain,
    output_bias,
    final_weight,
    final_bias,
):
    row_tile = pair_map.shape[0]
    row_count = lax.axis_size("row")
    col_count = lax.axis_size("col")
    total_rows = row_tile * row_count
    slab_total = SLAB_PER * col_count
    stride = total_rows // slab_total
    local_slab = pair_map[::stride]
    slab_normed = layer_norm(local_slab, input_gain, input_bias).astype(jnp.bfloat16)
    gate_value = jax.nn.sigmoid(linear(slab_normed, gate_weight, gate_bias))
    left_side = lax.all_gather(
        gated_linear(slab_normed, left_weight, left_bias), "row", axis=0, tiled=True
    )
    normed = layer_norm(pair_map, input_gain, input_bias).astype(jnp.bfloat16)
    right_side = gated_linear(normed, right_weight, right_bias)
    slab_share = slab_total // row_count
    slab_first = lax.axis_index("row") * slab_share
    summed_normed = layer_norm(
        lax.psum_scatter(
            jnp.einsum(
                "skh,jkh->sjh", left_side, right_side, preferred_element_type=jnp.float32
            ).astype(jnp.bfloat16),
            "col",
            scatter_dimension=0,
            tiled=True,
        ).astype(jnp.float32),
        output_gain,
        output_bias,
    ).astype(jnp.bfloat16)
    own_rows = linear(summed_normed, final_weight, final_bias).astype(jnp.bfloat16)
    spread = lax.all_gather(own_rows, "row", axis=1, tiled=True)
    arrived = lax.all_to_all(spread, "col", split_axis=1, concat_axis=0, tiled=True)
    update = lax.dynamic_slice_in_dim(arrived, slab_first, slab_share, 0)
    return (gate_value * update.astype(jnp.float32)).astype(jnp.bfloat16)


def solution(mesh):
    placed = (P("row", "col", None), P(), P(), P(), P(), P(), P(), P(), P(), P(), P(), P(), P())
    return jax.shard_map(
        body, mesh=mesh, in_specs=placed, out_specs=P("row", "col", None), check_vma=False
    )
```

profile of v0, /device:TPU:0, one launch (start us, length us, event | category | flops | bytes accessed | tf_op | source)
XLA Modules:
  0.0 143.1 jit_solution(8037428460084802292)
XLA Ops:
  6.6 3.6 %convert_reduce_fusion = f32[160,80]{1,0:T(8,128)S(1)} fusion(bf16[160,80,128]{2,1,0:T(8,128)(2,1)} %param.13), kind=kLoop, calls=%fused_computation.3 | loop fusion | flops 3264000 | bytes 3328000 | tf_op jit(solution)/shard_map/reduce_sum | solution.py:14
  10.2 0.9 convert_reduce_fusion.2
  11.1 5.9 %fusion.2 = f32[160,80]{1,0:T(8,128)S(1)} fusion(bf16[160,80,128]{2,1,0:T(8,128)(2,1)} %param.13, f32[160,80]{1,0:T(8,128)S(1)} %broadcast_multiply_fusion), kind=kLoop, calls=%fused_computation.6 | loop fusion | flops 6540800 | bytes 3379200 | tf_op jit(solution)/shard_map/reduce_sum | solution.py:15
  17.1 4.2 %fusion.5 = bf16[160,80,128]{2,1,0:T(8,128)(2,1)S(1)} fusion(bf16[160,80,128]{2,1,0:T(8,128)(2,1)S(1)} %copy-done.1, f32[128]{0:T(128)S(1)} %copy-done.4, f32[128]{0:T(128)S(1)} %copy-done.5, f32[160,80]{1,0:T(8,128)S(1)} %add_rsqrt_fusion, f32[160,80]{1,0:T(8,128)S(1)} %broadcast_multiply_fusion), kind=kLoop, calls=%fused_computation.9 | loop fusion | flops 9830400 | bytes 6657024 | tf_op jit(solution)/shard_map/convert_element_type | solution.py:58
  21.3 6.5 %convolution_add_fusion = f32[12800,256]{1,0:T(8,128)} fusion(bf16[12800,128]{1,0:T(8,128)(2,1)S(1)} %bitcast.28, bf16[128,256]{1,0:T(8,128)(2,1)S(1)} %copy-done, f32[256]{0:T(256)S(1)} %copy-done.3), kind=kOutput, calls=%fused_computation | convolution fusion | flops 842137600 | bytes 16450560 | tf_op jit(solution)/shard_map/dot_general | solution.py:21
  27.8 10.3 %fusion.38 = (f32[160,80,128]{2,1,0:T(8,128)}, f32[160,80,128]{2,1,0:T(8,128)}) fusion(f32[160,80,256]{2,1,0:T(8,128)} %bitcast.27), kind=kLoop, calls=%fused_computation.57 | loop fusion | bytes 26214400 | tf_op jit(solution)/shard_map/slice | solution.py:28
  38.1 9.7 %copy.34 = f32[160,80,128]{1,0,2:T(8,128)} copy(f32[160,80,128]{2,1,0:T(8,128)} %get-tuple-element.5) | data formatting | bytes 13107200
  47.8 9.8 %copy.35 = f32[160,80,128]{1,0,2:T(8,128)} copy(f32[160,80,128]{2,1,0:T(8,128)} %get-tuple-element.6) | data formatting | bytes 13107200
  58.2 10.1 %all_gather.6 = bf16[8,80,128]{2,1,0:T(8,128)(2,1)S(1)} all-gather(bf16[2,80,128]{2,1,0:T(8,128)(2,1)S(1)} %fusion.26), channel_id=1, replica_groups=mesh['row'=4,'col'=8] {'row'}, dimensions={0}, use_global_device_ids=true | all-gather | bytes 204800 | tf_op jit(solution)/shard_map/all_gather | solution.py:55
  68.2 0.2 copy.30
  68.5 9.8 %fusion.8 = bf16[8,160,128]{1,0,2:T(8,128)(2,1)S(1)} fusion(bf16[8,80,128]{1,0,2:T(8,128)(2,1)S(1)} %copy.30, f32[160,80,128]{1,0,2:T(8,128)} %copy.35, f32[160,80,128]{1,0,2:T(8,128)} %copy.34), kind=kOutput, calls=%fused_computation.12 | convolution fusion | flops 34570240 | bytes 13598720 | tf_op jit(solution)/shard_map/skh,jkh->sjh/dot_general | solution.py:64
  78.3 1.1 copy.31
  79.4 31.0 %reduce-scatter.2.cloned.1.call-done = bf16[1,160,128]{2,1,0:T(8,128)(2,1)} async-done(((bf16[8,160,128]{2,1,0:T(8,128)(2,1)}), bf16[1,160,128]{2,1,0:T(8,128)(2,1)}) %reduce-scatter.2.cloned.1.call-update) | async-done | bytes 40976 | tf_op jit(solution)/shard_map/reduce_scatter | solution.py:63
  110.4 0.9 convert_reduce_fusion.1
  111.3 1.0 fusion.18
  112.3 1.0 fusion.13
  113.3 8.5 %all-gather = bf16[640,128]{1,0:T(8,128)(2,1)S(1)} all-gather(bf16[160,128]{1,0:T(8,128)(2,1)S(1)} %fusion.13), channel_id=2, replica_groups=mesh['row'=4,'col'=8] {'row'}, dimensions={0}, use_global_device_ids=true | all-gather | bytes 204800 | tf_op jit(solution)/shard_map/all_gather | solution.py:75
  121.9 0.3 copy.37
  122.1 0.5 broadcast.104
  122.6 1.6 %reduce.2 = bf16[640,128]{1,0:T(8,128)(2,1)S(1)} reduce(bf16[640,1,128]{2,1,0:T(2,128)(2,1)S(1)} %bitcast.29, bf16[]{:T(256)} %broadcast.104), dimensions={1}, to_apply=%bitcast.26.reduce_sub_computation | reduce | bytes 327682
  124.2 0.7 reshape.95
  124.9 3.4 %all-to-all-start = ((bf16[8,2,5120]{2,1,0:T(2,128)(2,1)}), bf16[8,2,5120]{2,1,0:T(2,128)(2,1)S(1)}, u32[]{:S(2)}, u32[]{:S(2)}) async-start(bf16[8,2,5120]{2,1,0:T(2,128)(2,1)} %reshape.95), calls=%async_computation.1 | async-start | bytes 327680 | tf_op jit(solution)/shard_map/all_to_all | solution.py:76
  128.5 7.0 %all-to-all-done = bf16[8,2,5120]{2,1,0:T(2,128)(2,1)S(1)} async-done(((bf16[8,2,5120]{2,1,0:T(2,128)(2,1)}), bf16[8,2,5120]{2,1,0:T(2,128)(2,1)S(1)}, u32[]{:S(2)}, u32[]{:S(2)}) %all-to-all-start) | async-done | bytes 163872 | tf_op jit(solution)/shard_map/all_to_all | solution.py:76
  135.6 0.6 fusion.30
  (41 shorter events, 1.0 us)
Async XLA Ops:
  6.5 14.7 %copy-start = (bf16[128,256]{1,0:T(8,128)(2,1)S(1)}, bf16[128,256]{1,0:T(8,128)(2,1)}, u32[]{:S(2)}) copy-start(bf16[128,256]{1,0:T(8,128)(2,1)} %param.18) | copy-start | bytes 196612
  6.5 10.5 %copy-start.1 = (bf16[160,80,128]{2,1,0:T(8,128)(2,1)S(1)}, bf16[160,80,128]{2,1,0:T(8,128)(2,1)}, u32[]{:S(2)}) copy-start(bf16[160,80,128]{2,1,0:T(8,128)(2,1)} %param.13) | copy-start | bytes 9830404
  6.5 10.5 %copy-start.5 = (f32[128]{0:T(128)S(1)}, f32[128]{0:T(128)}, u32[]{:S(2)}) copy-start(f32[128]{0:T(128)} %param.14) | copy-start | bytes 1540
  6.5 10.5 %copy-start.4 = (f32[128]{0:T(128)S(1)}, f32[128]{0:T(128)}, u32[]{:S(2)}) copy-start(f32[128]{0:T(128)} %param.15) | copy-start | bytes 1540
  6.5 14.7 %copy-start.3 = (f32[256]{0:T(256)S(1)}, f32[256]{0:T(256)}, u32[]{:S(2)}) copy-start(f32[256]{0:T(256)} %param.19) | copy-start | bytes 3076
  6.5 103.8 %reduce-scatter.2.cloned.1.call-start = ((), (), s32[]{:S(2)}) async-start(), calls=%async_computation.2 | async-start | bytes 368640 | tf_op jit(solution)/shard_map/reduce_scatter | solution.py:63
  47.8 10.1 %copy-start.2 = (bf16[128,256]{1,0:T(8,128)(2,1)S(1)}, bf16[128,256]{1,0:T(8,128)(2,1)}, u32[]{:S(2)}) copy-start(bf16[128,256]{1,0:T(8,128)(2,1)} %param.16) | copy-start | bytes 196612
  47.8 10.1 %copy-start.6 = (f32[256]{0:T(256)S(1)}, f32[256]{0:T(256)}, u32[]{:S(2)}) copy-start(f32[256]{0:T(256)} %param.17) | copy-start | bytes 3076
  68.4 43.9 %copy-start.7 = (bf16[128,128]{1,0:T(8,128)(2,1)S(1)}, bf16[128,128]{1,0:T(8,128)(2,1)}, u32[]{:S(2)}) copy-start(bf16[128,128]{1,0:T(8,128)(2,1)} %param.24) | copy-start | bytes 98308
  68.4 43.9 %copy-start.9 = (f32[128]{0:T(128)S(1)}, f32[128]{0:T(128)}, u32[]{:S(2)}) copy-start(f32[128]{0:T(128)} %param.25) | copy-start | bytes 1540
  68.4 43.9 %copy-start.10 = (f32[128]{0:T(128)S(1)}, f32[128]{0:T(128)}, u32[]{:S(2)}) copy-start(f32[128]{0:T(128)} %param.23) | copy-start | bytes 1540
  68.4 43.9 %copy-start.11 = (f32[128]{0:T(128)S(1)}, f32[128]{0:T(128)}, u32[]{:S(2)}) copy-start(f32[128]{0:T(128)} %param.22) | copy-start | bytes 1540
  68.5 59.9 %copy-start.8 = (bf16[128,128]{1,0:T(8,128)(2,1)S(1)}, bf16[128,128]{1,0:T(8,128)(2,1)}, u32[]{:S(2)}) copy-start(bf16[128,128]{1,0:T(8,128)(2,1)} %param.20) | copy-start | bytes 98308
  68.5 59.9 %copy-start.12 = (f32[128]{0:T(128)S(1)}, f32[128]{0:T(128)}, u32[]{:S(2)}) copy-start(f32[128]{0:T(128)} %param.21) | copy-start | bytes 1540
  124.9 10.5 %all-to-all-start = ((bf16[8,2,5120]{2,1,0:T(2,128)(2,1)}), bf16[8,2,5120]{2,1,0:T(2,128)(2,1)S(1)}, u32[]{:S(2)}, u32[]{:S(2)}) async-start(bf16[8,2,5120]{2,1,0:T(2,128)(2,1)} %reshape.95), calls=%async_computation.1 | async-start | bytes 327680 | tf_op jit(solution)/shard_map/all_to_all | solution.py:76
Sparse Core Ops, SparseCore 0:
  79.5 30.8 reduce-scatter.1
where the time goes:
time: 144 us; the launch traced here: 143 us
  waiting for transfers between devices  37.9 us (26%)
  local copies, waits for them, and re-layouts  32.8 us (23%)
  other arithmetic  19 us (13%)
  blocking collectives  18.6 us (13%)
  matrix products  17.6 us (12%)
  between operations  13.7 us (10%)
  starting transfers between devices  3.42 us (2%)
    reduce_scatter x1, waiting for transfers between devices, body(): lax.psum_scatter(jnp.einsum('skh,jkh->sjh', left_side, right_side, prefer...  31 us
    unnamed x32, local copies, waits for them, and re-layouts  21 us
    slice x1, local copies, waits for them, and re-layouts, gated_linear(): joined[..., middle:]  10.3 us
    all_gather x1, blocking collectives, body(): lax.all_gather(gated_linear(slab_normed, left_weight, left_bias), 'row',...  10.1 us
    dot_general x1, matrix products, body(): jnp.einsum('skh,jkh->sjh', left_side, right_side, preferred_element_type=...  9.82 us
    all_gather x1, blocking collectives, body(): spread = lax.all_gather(own_rows, 'row', axis=1, tiled=True)  8.54 us
    dot_general x4, matrix products, linear(): jnp.dot(flattened, weight, preferred_element_type=jnp.float32) + offset  7.83 us
    reduce_sum x3, other arithmetic, layer_norm(): spread = jnp.mean(jnp.square(values - center), axis=-1, keepdims=True)  7.09 us
  transfers between devices with their start and end apart: 2, of which 2 were waited for; matrix products, arithmetic and copies ran while one was open for 0% of the time, Pallas kernels for 0%

commit v1 on v0

v1 whole, which is shorter than its diff:
```python
import functools

import jax
import jax.numpy as jnp
from jax import lax
from jax.experimental import pallas as pl
from jax.experimental.pallas import tpu as pltpu
from jax.sharding import PartitionSpec as P

SLAB_PER = 1
CHUNK = 16
STEP = 4
LAG = 3
LANES = 128

epsilon = 1e-05
MESH = pl.DeviceIdType.MESH


def norm_rows(x, ones, gain, bias):
    mean = jnp.dot(x, ones, preferred_element_type=jnp.float32)
    d = x.astype(jnp.float32) - mean
    var = jnp.dot((d * d).astype(jnp.bfloat16), ones, preferred_element_type=jnp.float32)
    return (d * lax.rsqrt(var + epsilon) * gain + bias).astype(jnp.bfloat16)


def gated(normed, half_weight, half_bias):
    z = jnp.dot(normed, half_weight, preferred_element_type=jnp.float32) + half_bias
    v = z[:, :LANES]
    return (v * jnp.tanh(z[:, LANES:]) + v).astype(jnp.bfloat16)


def kernel(
    row_count,
    col_count,
    slab_total,
    pair,
    input_gain,
    input_bias,
    left_weight,
    left_bias,
    right_weight,
    right_bias,
    gate_weight,
    gate_bias,
    output_gain,
    output_bias,
    final_weight,
    final_bias,
    out,
    x_buf,
    slab_buf,
    left,
    gate,
    right,
    half_right,
    msg,
    recv,
    x_sem,
    slab_sem,
    left_send,
    left_recv,
    part_send,
    part_recv,
):
    row_tile, col_tile, _ = pair.shape
    share = slab_total // row_count
    stride = row_tile * row_count // slab_total
    blocks = row_tile // col_tile
    per_block = col_tile // CHUNK
    chunks = row_tile // CHUNK
    r = lax.axis_index("row")
    c = lax.axis_index("col")

    slab_copies = []
    for i in range(share):
        cp = pltpu.make_async_copy(pair.at[i * stride], slab_buf.at[i], slab_sem.at[i])
        cp.start()
        slab_copies.append(cp)

    def x_copy(t):
        rows = pl.ds(t * CHUNK, CHUNK)
        return pltpu.make_async_copy(pair.at[rows], x_buf.at[rows], x_sem.at[t])

    def start_x(t, carry):
        x_copy(t).start()
        return carry

    lax.fori_loop(0, chunks, start_x, 0)

    barrier = pltpu.get_barrier_semaphore()
    for i in range(1, row_count):
        peer = lax.rem(r + i, row_count)
        pl.semaphore_signal(barrier, inc=1, device_id=(peer, c), device_id_type=MESH)
    source_row = c // blocks
    for i in range(col_count):

        @pl.when(jnp.logical_or(source_row != r, c != i))
        def _():
            pl.semaphore_signal(barrier, inc=1, device_id=(source_row, i), device_id_type=MESH)

    ones = jnp.full((LANES, LANES), 1.0 / LANES, jnp.bfloat16)
    gain, bias = input_gain[...], input_bias[...]
    half = jnp.bfloat16(0.5)
    half_right[...] = right_weight[...] * half
    half_right_bias = right_bias[...] * 0.5

    for cp in slab_copies:
        cp.wait()
    slab_rows = slab_buf[...].reshape(share * col_tile, LANES)
    slab_normed = norm_rows(slab_rows, ones, gain, bias)
    mine = gated(slab_normed, left_weight[...] * half, left_bias[...] * 0.5)
    left[r] = mine.reshape(share, col_tile, LANES)

    pl.semaphore_wait(
        barrier, row_count - 1 + row_count * blocks - (source_row == r).astype(jnp.int32)
    )

    left_copies = []
    for i in range(1, row_count):
        peer = lax.rem(r + i, row_count)
        cp = pltpu.make_async_remote_copy(
            src_ref=left.at[r],
            dst_ref=left.at[r],
            send_sem=left_send.at[i - 1],
            recv_sem=left_recv.at[i - 1],
            device_id=(peer, c),
            device_id_type=MESH,
        )
        cp.start()
        left_copies.append(cp)

    g = jnp.dot(slab_normed, gate_weight[...] * half, preferred_element_type=jnp.float32)
    gate[...] = (0.5 * jnp.tanh(g + gate_bias[...] * 0.5) + 0.5).reshape(share, col_tile, LANES)

    def project(t):
        for i in range(CHUNK // STEP):
            rows = pl.ds(t * CHUNK + i * STEP, STEP)
            x = x_buf[rows].reshape(STEP * col_tile, LANES)
            normed = norm_rows(x, ones, gain, bias)
            right[rows] = gated(normed, half_right[...], half_right_bias).reshape(
                STEP, col_tile, LANES
            )

    pick = (
        lax.broadcasted_iota(jnp.int32, (CHUNK, CHUNK * 16), 1) // 16
        == lax.broadcasted_iota(jnp.int32, (CHUNK, CHUNK * 16), 0)
    ).astype(jnp.bfloat16)

    def fold(p):
        parts = [p[i : i + 16] for i in range(0, col_tile, 16)]
        while len(parts) > 1:
            parts = [
                parts[i] + parts[i + 1] if i + 1 < len(parts) else parts[i]
                for i in range(0, len(parts), 2)
            ]
        return parts[0]

    def combine(t):
        def some(rr):
            for s in range(0, share, 2):
                group = range(s, min(s + 2, share))
                lefts = [left[rr, i] for i in group]
                sums = [[] for _ in group]
                for j in range(CHUNK):
                    row = right[t * CHUNK + j]
                    for n, values in enumerate(lefts):
                        sums[n].append(fold(values * row))
                for n, i in enumerate(group):
                    total = jnp.dot(
                        pick, jnp.concatenate(sums[n], 0), preferred_element_type=jnp.float32
                    )
                    msg[t, rr, i * CHUNK : (i + 1) * CHUNK, :] = total.astype(jnp.bfloat16)

        if row_count <= 4:
            for rr in range(row_count):
                some(rr)
        else:

            def step(rr, carry):
                some(rr)
                return carry

            lax.fori_loop(0, row_count, step, 0)

    def targets(t):
        target_col = r * blocks + t // per_block
        q = lax.rem(t, per_block)
        for rr in range(row_count):
            own = jnp.logical_and(r == rr, c == target_col)
            remote = pltpu.make_async_remote_copy(
                src_ref=msg.at[t, rr],
                dst_ref=recv.at[q, c],
                send_sem=part_send.at[t, rr],
                recv_sem=part_recv.at[q],
                device_id=(rr, target_col),
                device_id_type=MESH,
            )
            local = pltpu.make_async_copy(msg.at[t, rr], recv.at[q, c], part_recv.at[q])
            yield own, remote, local

    def send(t):
        for own, remote, local in targets(t):

            @pl.when(own)
            def _():
                local.start()

            @pl.when(jnp.logical_not(own))
            def _():
                remote.start()

    def project_only(t, carry):
        x_copy(t).wait()
        project(t)
        return carry

    def both(t, carry):
        x_copy(t).wait()
        project(t)
        combine(t - LAG)
        send(t - LAG)
        return carry

    def combine_only(t, carry):
        combine(t)
        send(t)
        return carry

    lax.fori_loop(0, LAG, project_only, 0)
    for cp in left_copies:
        cp.wait_recv()
    lax.fori_loop(LAG, chunks, both, 0)
    lax.fori_loop(chunks - LAG, chunks, combine_only, 0)

    out_gain, out_bias = output_gain[...], output_bias[...]

    def finish(q, carry):
        pltpu.make_async_copy(recv.at[q], recv.at[q], part_recv.at[q]).wait()
        total = jnp.sum(recv[q].astype(jnp.float32), axis=0)
        mean = jnp.mean(total, axis=-1, keepdims=True)
        d = total - mean
        var = jnp.mean(d * d, axis=-1, keepdims=True)
        normed = (d * lax.rsqrt(var + epsilon) * out_gain + out_bias).astype(jnp.bfloat16)
        update = jnp.dot(normed, final_weight[...], preferred_element_type=jnp.float32)
        update = (update + final_bias[...]).astype(jnp.bfloat16).astype(jnp.float32)
        cols = pl.ds(pl.multiple_of(q * CHUNK, CHUNK), CHUNK)
        for i in range(share):
            out[i, cols, :] = (
                gate[i, cols, :] * update[i * CHUNK : (i + 1) * CHUNK]
            ).astype(jnp.bfloat16)
        return carry

    lax.fori_loop(0, per_block, finish, 0)

    def drain(t, carry):
        for own, remote, _ in targets(t):

            @pl.when(jnp.logical_not(own))
            def _():
                remote.wait_send()

        return carry

    for cp in left_copies:
        cp.wait_send()
    lax.fori_loop(0, chunks, drain, 0)


def body(pair_map, *params):
    row_tile, col_tile, channels = pair_map.shape
    row_count = lax.axis_size("row")
    col_count = lax.axis_size("col")
    slab_total = SLAB_PER * col_count
    share = slab_total // row_count
    chunks = row_tile // CHUNK
    per_block = col_tile // CHUNK
    vmem = pl.BlockSpec(memory_space=pltpu.VMEM)
    params = [p.reshape(1, -1) if p.ndim == 1 else p for p in params]
    bf16, f32 = jnp.bfloat16, jnp.float32
    dma = pltpu.SemaphoreType.DMA
    rows = row_tile * col_tile
    return pl.pallas_call(
        functools.partial(kernel, row_count, col_count, slab_total),
        out_shape=jax.ShapeDtypeStruct((share, col_tile, channels), bf16),
        in_specs=[pl.BlockSpec(memory_space=pltpu.HBM)] + [vmem] * len(params),
        out_specs=vmem,
        scratch_shapes=[
            pltpu.VMEM((row_tile, col_tile, channels), bf16),
            pltpu.VMEM((share, col_tile, channels), bf16),
            pltpu.VMEM((row_count, share, col_tile, channels), bf16),
            pltpu.VMEM((share, col_tile, channels), f32),
            pltpu.VMEM((row_tile, col_tile, channels), bf16),
            pltpu.VMEM((channels, 2 * channels), bf16),
            pltpu.VMEM((chunks, row_count, share * CHUNK, channels), bf16),
            pltpu.VMEM((per_block, col_count, share * CHUNK, channels), bf16),
            dma((chunks,)),
            dma((share,)),
            dma((row_count - 1,)),
            dma((row_count - 1,)),
            dma((chunks, row_count)),
            dma((per_block,)),
        ],
        compiler_params=pltpu.CompilerParams(
            collective_id=0, has_side_effects=True, vmem_limit_bytes=48 * 1024 * 1024
        ),
        cost_estimate=pl.CostEstimate(
            flops=rows * channels * channels * 8,
            bytes_accessed=rows * channels * 2,
            transcendentals=rows * channels * 2,
        ),
        name="triangle_update",
    )(pair_map, *params)


def solution(mesh):
    placed = (P("row", "col", None),) + (P(),) * 12
    return jax.shard_map(
        body, mesh=mesh, in_specs=placed, out_specs=P("row", "col", None), check_vma=False
    )
```

time: 144 us -> 46.3 us (0.32)
  the two profiles are of different devices: /device:TPU:0 before, /device:TPU:1 now
where the time goes in v1:
time: 46.3 us; the launch traced here: 45.8 us
  Pallas kernels  34.8 us (75%)
  local copies, waits for them, and re-layouts  11 us (24%)
    pallas_call x1, Pallas kernels, body(): pl.pallas_call(functools.partial(kernel, row_count, col_count, slab_total...  34.8 us
    unnamed x27, local copies, waits for them, and re-layouts  11 us

profile of v1, /device:TPU:1, one launch (start us, length us, event | category | flops | bytes accessed | tf_op | source)
XLA Modules:
  0.0 45.8 jit_solution(8220491786545165246)
XLA Ops:
  0.0 0.0 copy-start
  0.0 1.9 %copy-done = bf16[160,80,128]{2,1,0:T(8,128)(2,1)S(1)} copy-done((bf16[160,80,128]{2,1,0:T(8,128)(2,1)S(1)}, bf16[160,80,128]{2,1,0:T(8,128)(2,1)}, u32[]{:S(2)}) %copy-start) | copy-done | bytes 3276824
  1.9 0.0 copy-start.1
  1.9 0.8 %copy-done.1 = bf16[128,256]{1,0:T(8,128)(2,1)S(1)} copy-done((bf16[128,256]{1,0:T(8,128)(2,1)S(1)}, bf16[128,256]{1,0:T(8,128)(2,1)}, u32[]{:S(2)}) %copy-start.1) | copy-done | bytes 65560
  2.8 0.0 copy-start.2
  2.8 0.8 %copy-done.2 = bf16[128,256]{1,0:T(8,128)(2,1)S(1)} copy-done((bf16[128,256]{1,0:T(8,128)(2,1)S(1)}, bf16[128,256]{1,0:T(8,128)(2,1)}, u32[]{:S(2)}) %copy-start.2) | copy-done | bytes 65560
  3.6 0.0 copy-start.3
  3.6 0.8 %copy-done.3 = bf16[128,128]{1,0:T(8,128)(2,1)S(1)} copy-done((bf16[128,128]{1,0:T(8,128)(2,1)S(1)}, bf16[128,128]{1,0:T(8,128)(2,1)}, u32[]{:S(2)}) %copy-start.3) | copy-done | bytes 32792
  4.4 0.0 copy-start.4
  4.4 0.8 %copy-done.4 = bf16[128,128]{1,0:T(8,128)(2,1)S(1)} copy-done((bf16[128,128]{1,0:T(8,128)(2,1)S(1)}, bf16[128,128]{1,0:T(8,128)(2,1)}, u32[]{:S(2)}) %copy-start.4) | copy-done | bytes 32792
  5.1 0.0 copy-start.5
  5.1 0.7 %copy-done.5 = f32[256]{0:T(256)S(1)} copy-done((f32[256]{0:T(256)S(1)}, f32[256]{0:T(256)}, u32[]{:S(2)}) %copy-start.5) | copy-done | bytes 1048
  5.8 0.0 copy-start.6
  5.8 0.7 %copy-done.6 = f32[256]{0:T(256)S(1)} copy-done((f32[256]{0:T(256)S(1)}, f32[256]{0:T(256)}, u32[]{:S(2)}) %copy-start.6) | copy-done | bytes 1048
  6.5 0.0 copy-start.7
  6.5 0.7 %copy-done.7 = f32[128]{0:T(128)S(1)} copy-done((f32[128]{0:T(128)S(1)}, f32[128]{0:T(128)}, u32[]{:S(2)}) %copy-start.7) | copy-done | bytes 536
  7.1 0.0 copy-start.8
  7.1 0.7 %copy-done.8 = f32[128]{0:T(128)S(1)} copy-done((f32[128]{0:T(128)S(1)}, f32[128]{0:T(128)}, u32[]{:S(2)}) %copy-start.8) | copy-done | bytes 536
  7.8 0.7 %copy-done.9 = f32[128]{0:T(128)S(1)} copy-done((f32[128]{0:T(128)S(1)}, f32[128]{0:T(128)}, u32[]{:S(2)}) %copy-start.9) | copy-done | bytes 536
  8.5 0.7 %copy-done.10 = f32[128]{0:T(128)S(1)} copy-done((f32[128]{0:T(128)S(1)}, f32[128]{0:T(128)}, u32[]{:S(2)}) %copy-start.10) | copy-done | bytes 536
  9.1 0.7 %copy-done.11 = f32[128]{0:T(128)S(1)} copy-done((f32[128]{0:T(128)S(1)}, f32[128]{0:T(128)}, u32[]{:S(2)}) %copy-start.11) | copy-done | bytes 536
  9.8 0.7 %copy-done.12 = f32[128]{0:T(128)S(1)} copy-done((f32[128]{0:T(128)S(1)}, f32[128]{0:T(128)}, u32[]{:S(2)}) %copy-start.12) | copy-done | bytes 536
  10.4 34.8 %triangle_update.1 = bf16[2,80,128]{2,1,0:T(8,128)(2,1)S(1)} custom-call(bf16[160,80,128]{2,1,0:T(8,128)(2,1)S(1)} %copy-done, f32[1,128]{1,0:T(1,128)S(1)} %bitcast.10, f32[1,128]{1,0:T(1,128)S(1)} %bitcast.11, bf16[128,256]{1,0:T(8,128)(2,1)S(1)} %copy-done.1, f32[1,256]{1,0:T(1,128)S(1)} %bitcast.8, bf16[128,256]{1,0:T(8,128)(2,1)S(1)} %copy-done.2, ...), custom_call_target="tpu_custom_call" | custom-call | flops 1677721600 | bytes 3276800 | tf_op jit(solution)/shard_map/triangle_update/pallas_call | solution.py:283
  45.2 0.6 %copy.15 = bf16[2,80,128]{2,1,0:T(8,128)(2,1)} copy(bf16[2,80,128]{2,1,0:T(8,128)(2,1)S(1)} %triangle_update.1) | data formatting | bytes 81920
  (4 shorter events, 0.0 us)
Async XLA Ops:
  0.0 1.9 %copy-start = (bf16[160,80,128]{2,1,0:T(8,128)(2,1)S(1)}, bf16[160,80,128]{2,1,0:T(8,128)(2,1)}, u32[]{:S(2)}) copy-start(bf16[160,80,128]{2,1,0:T(8,128)(2,1)} %pair.1) | copy-start | bytes 9830404
  1.9 0.8 %copy-start.1 = (bf16[128,256]{1,0:T(8,128)(2,1)S(1)}, bf16[128,256]{1,0:T(8,128)(2,1)}, u32[]{:S(2)}) copy-start(bf16[128,256]{1,0:T(8,128)(2,1)} %left_weight.1) | copy-start | bytes 196612
  2.8 0.8 %copy-start.2 = (bf16[128,256]{1,0:T(8,128)(2,1)S(1)}, bf16[128,256]{1,0:T(8,128)(2,1)}, u32[]{:S(2)}) copy-start(bf16[128,256]{1,0:T(8,128)(2,1)} %right_weight.1) | copy-start | bytes 196612
  3.6 0.8 %copy-start.3 = (bf16[128,128]{1,0:T(8,128)(2,1)S(1)}, bf16[128,128]{1,0:T(8,128)(2,1)}, u32[]{:S(2)}) copy-start(bf16[128,128]{1,0:T(8,128)(2,1)} %gate_weight.1) | copy-start | bytes 98308
  4.4 0.8 %copy-start.4 = (bf16[128,128]{1,0:T(8,128)(2,1)S(1)}, bf16[128,128]{1,0:T(8,128)(2,1)}, u32[]{:S(2)}) copy-start(bf16[128,128]{1,0:T(8,128)(2,1)} %final_weight.1) | copy-start | bytes 98308
  5.1 0.7 %copy-start.5 = (f32[256]{0:T(256)S(1)}, f32[256]{0:T(256)}, u32[]{:S(2)}) copy-start(f32[256]{0:T(256)} %param.17) | copy-start | bytes 3076
  5.8 0.7 %copy-start.6 = (f32[256]{0:T(256)S(1)}, f32[256]{0:T(256)}, u32[]{:S(2)}) copy-start(f32[256]{0:T(256)} %param.19) | copy-start | bytes 3076
  6.5 0.7 %copy-start.7 = (f32[128]{0:T(128)S(1)}, f32[128]{0:T(128)}, u32[]{:S(2)}) copy-start(f32[128]{0:T(128)} %param.14) | copy-start | bytes 1540
  7.1 0.7 %copy-start.8 = (f32[128]{0:T(128)S(1)}, f32[128]{0:T(128)}, u32[]{:S(2)}) copy-start(f32[128]{0:T(128)} %param.15) | copy-start | bytes 1540
  7.8 0.7 %copy-start.9 = (f32[128]{0:T(128)S(1)}, f32[128]{0:T(128)}, u32[]{:S(2)}) copy-start(f32[128]{0:T(128)} %param.21) | copy-start | bytes 1540
  8.5 0.7 %copy-start.10 = (f32[128]{0:T(128)S(1)}, f32[128]{0:T(128)}, u32[]{:S(2)}) copy-start(f32[128]{0:T(128)} %param.22) | copy-start | bytes 1540
  9.1 0.7 %copy-start.11 = (f32[128]{0:T(128)S(1)}, f32[128]{0:T(128)}, u32[]{:S(2)}) copy-start(f32[128]{0:T(128)} %param.23) | copy-start | bytes 1540
  9.8 0.7 %copy-start.12 = (f32[128]{0:T(128)S(1)}, f32[128]{0:T(128)}, u32[]{:S(2)}) copy-start(f32[128]{0:T(128)} %param.25) | copy-start | bytes 1540

commit v2 on v1

v2 whole, which is shorter than its diff:
```python
import functools

import jax
import jax.numpy as jnp
from jax import lax
from jax.experimental import pallas as pl
from jax.experimental.pallas import tpu as pltpu
from jax.sharding import PartitionSpec as P

SLAB_PER = 1
CHUNK = 16
STEP = 4
LAG = 3
FORWARD_LAG = 2
LANES = 128

epsilon = 1e-05
MESH = pl.DeviceIdType.MESH


def norm_rows(x, ones, gain, bias):
    mean = jnp.dot(x, ones, preferred_element_type=jnp.float32)
    d = x.astype(jnp.float32) - mean
    var = jnp.dot((d * d).astype(jnp.bfloat16), ones, preferred_element_type=jnp.float32)
    return (d * lax.rsqrt(var + epsilon) * gain + bias).astype(jnp.bfloat16)


def gated(normed, half_weight, half_bias):
    z = jnp.dot(normed, half_weight, preferred_element_type=jnp.float32) + half_bias
    v = z[:, :LANES]
    return (v * jnp.tanh(z[:, LANES:]) + v).astype(jnp.bfloat16)


def kernel(
    row_count,
    col_count,
    slab_total,
    pair,
    *refs,
):
    params, out, refs = refs[:12], refs[12], refs[13:]
    held, refs = refs[:12], refs[12:]
    (
        x_buf,
        slab_buf,
        left,
        gate,
        right,
        half_right,
        pair_out,
        pair_in,
        chip_sum,
        spread,
        arrived,
        param_sem,
        x_sem,
        slab_sem,
        left_send,
        left_recv,
        pair_send,
        pair_recv,
        spread_send,
        spread_recv,
        forward_send,
        forward_recv,
    ) = refs
    (
        input_gain,
        input_bias,
        left_weight,
        left_bias,
        right_weight,
        right_bias,
        gate_weight,
        gate_bias,
        output_gain,
        output_bias,
        final_weight,
        final_bias,
    ) = held
    row_tile, col_tile, _ = pair.shape
    assert row_tile == 2 * col_tile and col_count == 2 * row_count
    share = slab_total // row_count
    stride = row_tile * row_count // slab_total
    blocks = row_tile // col_tile
    per_block = col_tile // CHUNK
    chunks = row_tile // CHUNK
    r = lax.axis_index("row")
    c = lax.axis_index("col")
    core = lax.rem(c, 2)
    chip = c // 2

    slab_copies = []
    for i in range(share):
        cp = pltpu.make_async_copy(pair.at[i * stride], slab_buf.at[i], slab_sem.at[i])
        cp.start()
        slab_copies.append(cp)
    param_copies = []
    for i in range(12):
        cp = pltpu.make_async_copy(params[i], held[i], param_sem.at[i])
        cp.start()
        param_copies.append(cp)

    def x_copy(t):
        rows = pl.ds(t * CHUNK, CHUNK)
        return pltpu.make_async_copy(pair.at[rows], x_buf.at[rows], x_sem.at[t])

    first_block = (1 - core) * per_block
    for start in (first_block, core * per_block):

        def start_x(q, carry):
            x_copy(start + q).start()
            return carry

        lax.fori_loop(0, per_block, start_x, 0)

    barrier = pltpu.get_barrier_semaphore()
    for i in range(1, row_count):
        peer = lax.rem(r + i, row_count)
        pl.semaphore_signal(barrier, inc=1, device_id=(peer, c), device_id_type=MESH)
    pl.semaphore_signal(barrier, inc=1, device_id=(r, c + 1 - 2 * core), device_id_type=MESH)
    for i in range(col_count // 2):

        @pl.when(chip != i)
        def _():
            pl.semaphore_signal(
                barrier, inc=1, device_id=(r, 2 * i + core), device_id_type=MESH
            )

    for cp in param_copies:
        cp.wait()
    ones = jnp.full((LANES, LANES), 1.0 / LANES, jnp.bfloat16)
    gain, bias = input_gain[...], input_bias[...]
    half = jnp.bfloat16(0.5)
    half_right[...] = right_weight[...] * half
    half_right_bias = right_bias[...] * 0.5

    for cp in slab_copies:
        cp.wait()
    slab_rows = slab_buf[...].reshape(share * col_tile, LANES)
    slab_normed = norm_rows(slab_rows, ones, gain, bias)
    mine = gated(slab_normed, left_weight[...] * half, left_bias[...] * 0.5)
    left[r] = mine.reshape(share, col_tile, LANES)

    pl.semaphore_wait(barrier, row_count - 1 + 1 + col_count // 2 - 1)

    left_copies = []
    for i in range(1, row_count):
        peer = lax.rem(r + i, row_count)
        cp = pltpu.make_async_remote_copy(
            src_ref=left.at[r],
            dst_ref=left.at[r],
            send_sem=left_send.at[i - 1],
            recv_sem=left_recv.at[i - 1],
            device_id=(peer, c),
            device_id_type=MESH,
        )
        cp.start()
        left_copies.append(cp)

    g = jnp.dot(slab_normed, gate_weight[...] * half, preferred_element_type=jnp.float32)
    gate[...] = (0.5 * jnp.tanh(g + gate_bias[...] * 0.5) + 0.5).reshape(share, col_tile, LANES)

    def row_chunk(u):
        block = jnp.where(u < per_block, 1 - core, core)
        return block * per_block + lax.rem(u, per_block)

    def project(u):
        t = row_chunk(u)
        x_copy(t).wait()
        for i in range(CHUNK // STEP):
            rows = pl.ds(t * CHUNK + i * STEP, STEP)
            x = x_buf[rows].reshape(STEP * col_tile, LANES)
            normed = norm_rows(x, ones, gain, bias)
            right[rows] = gated(normed, half_right[...], half_right_bias).reshape(
                STEP, col_tile, LANES
            )

    pick = (
        lax.broadcasted_iota(jnp.int32, (CHUNK, CHUNK * 16), 1) // 16
        == lax.broadcasted_iota(jnp.int32, (CHUNK, CHUNK * 16), 0)
    ).astype(jnp.bfloat16)

    def fold(p):
        parts = [p[i : i + 16] for i in range(0, col_tile, 16)]
        while len(parts) > 1:
            parts = [
                parts[i] + parts[i + 1] if i + 1 < len(parts) else parts[i]
                for i in range(0, len(parts), 2)
            ]
        return parts[0]

    def combine(u, put):
        first = row_chunk(u) * CHUNK

        def some(rr):
            for s in range(0, share, 2):
                group = range(s, min(s + 2, share))
                lefts = [left[rr, i] for i in group]
                sums = [[] for _ in group]
                for j in range(CHUNK):
                    row = right[first + j]
                    for n, values in enumerate(lefts):
                        sums[n].append(fold(values * row))
                for n, i in enumerate(group):
                    total = jnp.dot(
                        pick, jnp.concatenate(sums[n], 0), preferred_element_type=jnp.float32
                    )
                    put(rr, slice(i * CHUNK, (i + 1) * CHUNK), total)

        if row_count <= 4:
            for rr in range(row_count):
                some(rr)
        else:

            def step(rr, carry):
                some(rr)
                return carry

            lax.fori_loop(0, row_count, step, 0)

    def pair_copy(q):
        return pltpu.make_async_remote_copy(
            src_ref=pair_out.at[q],
            dst_ref=pair_in.at[q],
            send_sem=pair_send.at[q],
            recv_sem=pair_recv.at[q],
            device_id=(r, c + 1 - 2 * core),
            device_id_type=MESH,
        )

    def spread_copy(q, rr):
        return pltpu.make_async_remote_copy(
            src_ref=chip_sum.at[q, rr],
            dst_ref=spread.at[q, r],
            send_sem=spread_send.at[q, rr],
            recv_sem=spread_recv.at[q],
            device_id=(rr, c),
            device_id_type=MESH,
        )

    def forward_copy(q, source):
        return pltpu.make_async_remote_copy(
            src_ref=spread.at[q, source],
            dst_ref=arrived.at[q, chip],
            send_sem=forward_send.at[q, source],
            recv_sem=forward_recv.at[q],
            device_id=(r, source * blocks + core),
            device_id_type=MESH,
        )

    def for_others(count, own, act):
        for i in range(count):
            pl.when(own != i)(functools.partial(act, i))

    def combine_other(v):
        def put(rr, rows, total):
            pair_out[v, rr, rows, :] = total.astype(jnp.bfloat16)

        combine(v, put)
        pair_copy(v).start()

    def combine_own(v):
        q = v - per_block
        pair_copy(q).wait_recv()

        def put(rr, rows, total):
            both_cores = total + pair_in[q, rr, rows, :].astype(jnp.float32)
            chip_sum[q, rr, rows, :] = both_cores.astype(jnp.bfloat16)

        combine(v, put)
        for_others(row_count, r, lambda rr: spread_copy(q, rr).start())
        spread[q, r] = chip_sum[q, r]

    def forward(q):
        landed = spread.at[q, pl.ds(0, row_count - 1)]
        pltpu.make_async_copy(landed, landed, spread_recv.at[q]).wait()
        for_others(row_count, chip, lambda source: forward_copy(q, source).start())
        arrived[q, chip] = spread[q, chip]

    def loop(first, last, step):
        def run(v, carry):
            step(v)
            return carry

        lax.fori_loop(first, last, run, 0)

    def early(v):
        project(v + LAG)
        combine_other(v)

    def late(v):
        project(v + LAG)
        combine_own(v)

    def last(v):
        combine_own(v)

        @pl.when(v >= per_block + FORWARD_LAG)
        def _():
            forward(v - per_block - FORWARD_LAG)

    loop(0, LAG, project)
    for cp in left_copies:
        cp.wait_recv()
    loop(0, per_block, early)
    loop(per_block, chunks - LAG, late)
    loop(chunks - LAG, chunks, last)
    loop(per_block - FORWARD_LAG, per_block, forward)

    out_gain, out_bias = output_gain[...], output_bias[...]

    def finish(q, carry):
        landed = arrived.at[q, pl.ds(0, col_count // blocks - 1)]
        pltpu.make_async_copy(landed, landed, forward_recv.at[q]).wait()
        total = jnp.sum(arrived[q].astype(jnp.float32), axis=0)
        mean = jnp.mean(total, axis=-1, keepdims=True)
        d = total - mean
        var = jnp.mean(d * d, axis=-1, keepdims=True)
        normed = (d * lax.rsqrt(var + epsilon) * out_gain + out_bias).astype(jnp.bfloat16)
        update = jnp.dot(normed, final_weight[...], preferred_element_type=jnp.float32)
        update = (update + final_bias[...]).astype(jnp.bfloat16).astype(jnp.float32)
        cols = pl.ds(pl.multiple_of(q * CHUNK, CHUNK), CHUNK)
        for i in range(share):
            out[i, cols, :] = (
                gate[i, cols, :] * update[i * CHUNK : (i + 1) * CHUNK]
            ).astype(jnp.bfloat16)
        return carry

    lax.fori_loop(0, per_block, finish, 0)

    for cp in left_copies:
        cp.wait_send()

    def drain(q):
        pair_copy(q).wait_send()
        for_others(row_count, r, lambda rr: spread_copy(q, rr).wait_send())
        for_others(row_count, chip, lambda source: forward_copy(q, source).wait_send())

    loop(0, per_block, drain)


def body(pair_map, *params):
    row_tile, col_tile, channels = pair_map.shape
    row_count = lax.axis_size("row")
    col_count = lax.axis_size("col")
    slab_total = SLAB_PER * col_count
    share = slab_total // row_count
    chunks = row_tile // CHUNK
    per_block = col_tile // CHUNK
    vmem = pl.BlockSpec(memory_space=pltpu.VMEM)
    params = [p.reshape(1, -1) if p.ndim == 1 else p for p in params]
    bf16, f32 = jnp.bfloat16, jnp.float32
    dma = pltpu.SemaphoreType.DMA
    rows = row_tile * col_tile
    return pl.pallas_call(
        functools.partial(kernel, row_count, col_count, slab_total),
        out_shape=jax.ShapeDtypeStruct((share, col_tile, channels), bf16),
        in_specs=[pl.BlockSpec(memory_space=pltpu.HBM)] * (1 + len(params)),
        out_specs=vmem,
        scratch_shapes=[pltpu.VMEM(p.shape, p.dtype) for p in params]
        + [
            pltpu.VMEM((row_tile, col_tile, channels), bf16),
            pltpu.VMEM((share, col_tile, channels), bf16),
            pltpu.VMEM((row_count, share, col_tile, channels), bf16),
            pltpu.VMEM((share, col_tile, channels), f32),
            pltpu.VMEM((row_tile, col_tile, channels), bf16),
            pltpu.VMEM((channels, 2 * channels), bf16),
            pltpu.VMEM((per_block, row_count, share * CHUNK, channels), bf16),
            pltpu.VMEM((per_block, row_count, share * CHUNK, channels), bf16),
            pltpu.VMEM((per_block, row_count, share * CHUNK, channels), bf16),
            pltpu.VMEM((per_block, row_count, share * CHUNK, channels), bf16),
            pltpu.VMEM((per_block, col_count // 2, share * CHUNK, channels), bf16),
            dma((len(params),)),
            dma((chunks,)),
            dma((share,)),
            dma((row_count - 1,)),
            dma((row_count - 1,)),
            dma((per_block,)),
            dma((per_block,)),
            dma((per_block, row_count)),
            dma((per_block,)),
            dma((per_block, row_count)),
            dma((per_block,)),
        ],
        compiler_params=pltpu.CompilerParams(
            collective_id=0, has_side_effects=True, vmem_limit_bytes=60 * 1024 * 1024
        ),
        cost_estimate=pl.CostEstimate(
            flops=rows * channels * channels * 8,
            bytes_accessed=rows * channels * 2,
            transcendentals=rows * channels * 2,
        ),
        name="triangle_update",
    )(pair_map, *params)


def solution(mesh):
    placed = (P("row", "col", None),) + (P(),) * 12
    return jax.shard_map(
        body, mesh=mesh, in_specs=placed, out_specs=P("row", "col", None), check_vma=False
    )
```

time: 46.3 us -> 32.9 us (0.71)
  the two profiles are of different devices: /device:TPU:1 before, /device:TPU:0 now
where the time goes in v2:
time: 32.9 us; the launch traced here: 32.7 us
  Pallas kernels  31.3 us (95%)
  local copies, waits for them, and re-layouts  1.4 us (4%)
    pallas_call x1, Pallas kernels, body(): pl.pallas_call(functools.partial(kernel, row_count, col_count, slab_total...  31.3 us
    unnamed x1, local copies, waits for them, and re-layouts  1.4 us

profile of v2, /device:TPU:0, one launch (start us, length us, event | category | flops | bytes accessed | tf_op | source)
XLA Modules:
  0.0 32.7 jit_solution(1786634068210216224)
XLA Ops:
  0.0 31.3 %triangle_update.1 = bf16[2,80,128]{2,1,0:T(8,128)(2,1)} custom-call(bf16[160,80,128]{2,1,0:T(8,128)(2,1)} %pair.1, f32[1,128]{1,0:T(1,128)} %bitcast.10, f32[1,128]{1,0:T(1,128)} %bitcast.11, bf16[128,256]{1,0:T(8,128)(2,1)} %refs_2_.1, f32[1,256]{1,0:T(1,128)} %bitcast.8, bf16[128,256]{1,0:T(8,128)(2,1)} %refs_4_.1, f32[1,256]{1,0:T(1,128)} %bitcast.9, ...), custom_call_target="tpu_custom_call" | custom-call | flops 1677721600 | bytes 3276800 | tf_op jit(solution)/shard_map/triangle_update/pallas_call | solution.py:356
  31.3 1.4 %copy.15 = bf16[2,80,128]{2,1,0:T(8,128)(2,1)} copy(bf16[2,80,128]{2,1,0:T(8,128)(2,1)} %triangle_update.1) | data formatting | bytes 81920

commit v3 on v2

--- a/solution.py
+++ b/solution.py
@@ -9,18 +9,18 @@
 
 SLAB_PER = 1
 CHUNK = 16
-STEP = 4
-LAG = 3
-FORWARD_LAG = 2
+STEP = 8
+BEFORE = 3
+PAIR_LAG = 2
+FORWARD_LAG = 3
 LANES = 128
 
 epsilon = 1e-05
 MESH = pl.DeviceIdType.MESH
 
 
-def norm_rows(x, ones, gain, bias):
-    mean = jnp.dot(x, ones, preferred_element_type=jnp.float32)
-    d = x.astype(jnp.float32) - mean
+def norm_rows(x, center, ones, gain, bias):
+    d = jnp.dot(x, center, preferred_element_type=jnp.float32)
     var = jnp.dot((d * d).astype(jnp.bfloat16), ones, preferred_element_type=jnp.float32)
     return (d * lax.rsqrt(var + epsilon) * gain + bias).astype(jnp.bfloat16)
 
@@ -130,6 +130,8 @@
     for cp in param_copies:
         cp.wait()
     ones = jnp.full((LANES, LANES), 1.0 / LANES, jnp.bfloat16)
+    lane = [lax.broadcasted_iota(jnp.int32, (LANES, LANES), i) for i in range(2)]
+    center = (jnp.where(lane[0] == lane[1], 1.0, 0.0) - 1.0 / LANES).astype(jnp.bfloat16)
     gain, bias = input_gain[...], input_bias[...]
     half = jnp.bfloat16(0.5)
     half_right[...] = right_weight[...] * half
@@ -138,25 +140,9 @@
     for cp in slab_copies:
         cp.wait()
     slab_rows = slab_buf[...].reshape(share * col_tile, LANES)
-    slab_normed = norm_rows(slab_rows, ones, gain, bias)
+    slab_normed = norm_rows(slab_rows, center, ones, gain, bias)
     mine = gated(slab_normed, left_weight[...] * half, left_bias[...] * 0.5)
     left[r] = mine.reshape(share, col_tile, LANES)
-
-    pl.semaphore_wait(barrier, row_count - 1 + 1 + col_count // 2 - 1)
-
-    left_copies = []
-    for i in range(1, row_count):
-        peer = lax.rem(r + i, row_count)
-        cp = pltpu.make_async_remote_copy(
-            src_ref=left.at[r],
-            dst_ref=left.at[r],
-            send_sem=left_send.at[i - 1],
-            recv_sem=left_recv.at[i - 1],
-            device_id=(peer, c),
-            device_id_type=MESH,
-        )
-        cp.start()
-        left_copies.append(cp)
 
     g = jnp.dot(slab_normed, gate_weight[...] * half, preferred_element_type=jnp.float32)
     gate[...] = (0.5 * jnp.tanh(g + gate_bias[...] * 0.5) + 0.5).reshape(share, col_tile, LANES)
@@ -171,7 +157,7 @@
         for i in range(CHUNK // STEP):
             rows = pl.ds(t * CHUNK + i * STEP, STEP)
             x = x_buf[rows].reshape(STEP * col_tile, LANES)
-            normed = norm_rows(x, ones, gain, bias)
+            normed = norm_rows(x, center, ones, gain, bias)
             right[rows] = gated(normed, half_right[...], half_right_bias).reshape(
                 STEP, col_tile, LANES
             )
@@ -260,15 +246,14 @@
         combine(v, put)
         pair_copy(v).start()
 
-    def combine_own(v):
-        q = v - per_block
+    def combine_own(q):
         pair_copy(q).wait_recv()
 
         def put(rr, rows, total):
             both_cores = total + pair_in[q, rr, rows, :].astype(jnp.float32)
             chip_sum[q, rr, rows, :] = both_cores.astype(jnp.bfloat16)
 
-        combine(v, put)
+        combine(q + per_block, put)
         for_others(row_count, r, lambda rr: spread_copy(q, rr).start())
         spread[q, r] = chip_sum[q, r]
 
@@ -286,26 +271,42 @@
         lax.fori_loop(first, last, run, 0)
 
     def early(v):
-        project(v + LAG)
         combine_other(v)
 
-    def late(v):
-        project(v + LAG)
-        combine_own(v)
-
-    def last(v):
-        combine_own(v)
-
-        @pl.when(v >= per_block + FORWARD_LAG)
+    def middle(v):
+        combine_other(v)
+        late(v - PAIR_LAG)
+
+    def late(q):
+        combine_own(q)
+
+        @pl.when(q >= FORWARD_LAG)
         def _():
-            forward(v - per_block - FORWARD_LAG)
-
-    loop(0, LAG, project)
+            forward(q - FORWARD_LAG)
+
+    loop(0, BEFORE, project)
+    pl.semaphore_wait(barrier, row_count - 1 + 1 + col_count // 2 - 1)
+
+    left_copies = []
+    for i in range(1, row_count):
+        peer = lax.rem(r + i, row_count)
+        cp = pltpu.make_async_remote_copy(
+            src_ref=left.at[r],
+            dst_ref=left.at[r],
+            send_sem=left_send.at[i - 1],
+            recv_sem=left_recv.at[i - 1],
+            device_id=(peer, c),
+            device_id_type=MESH,
+        )
+        cp.start()
+        left_copies.append(cp)
+
+    loop(BEFORE, chunks, project)
     for cp in left_copies:
         cp.wait_recv()
-    loop(0, per_block, early)
-    loop(per_block, chunks - LAG, late)
-    loop(chunks - LAG, chunks, last)
+    loop(0, PAIR_LAG, early)
+    loop(PAIR_LAG, per_block, middle)
+    loop(per_block - PAIR_LAG, per_block, late)
     loop(per_block - FORWARD_LAG, per_block, forward)
 
     out_gain, out_bias = output_gain[...], output_bias[...]

time: 32.9 us -> 27.9 us (0.85)
  Pallas kernels: 31.3 us -> 26.3 us
    pallas_call x1, Pallas kernels: 31.3 us -> 26.3 us  [body(): pl.pallas_call(functools.partial(kernel, row_count, col_count, slab_total...]
where the time goes in v3:
time: 27.9 us; the launch traced here: 27.7 us
  Pallas kernels  26.3 us (94%)
  local copies, waits for them, and re-layouts  1.4 us (5%)
    pallas_call x1, Pallas kernels, body(): pl.pallas_call(functools.partial(kernel, row_count, col_count, slab_total...  26.3 us
    unnamed x1, local copies, waits for them, and re-layouts  1.4 us

profile of v3, /device:TPU:0, one launch (start us, length us, event | category | flops | bytes accessed | tf_op | source)
XLA Modules:
  0.0 27.7 jit_solution(13895171456895469243)
XLA Ops:
  0.0 26.3 %triangle_update.1 = bf16[2,80,128]{2,1,0:T(8,128)(2,1)} custom-call(bf16[160,80,128]{2,1,0:T(8,128)(2,1)} %pair.1, f32[1,128]{1,0:T(1,128)} %bitcast.10, f32[1,128]{1,0:T(1,128)} %bitcast.11, bf16[128,256]{1,0:T(8,128)(2,1)} %refs_2_.1, f32[1,256]{1,0:T(1,128)} %bitcast.8, bf16[128,256]{1,0:T(8,128)(2,1)} %refs_4_.1, f32[1,256]{1,0:T(1,128)} %bitcast.9, ...), custom_call_target="tpu_custom_call" | custom-call | flops 1677721600 | bytes 3276800 | tf_op jit(solution)/shard_map/triangle_update/pallas_call | solution.py:357
  26.3 1.4 %copy.15 = bf16[2,80,128]{2,1,0:T(8,128)(2,1)} copy(bf16[2,80,128]{2,1,0:T(8,128)(2,1)} %triangle_update.1) | data formatting | bytes 81920
